TPU v7x, 32 devices: a whole 2x2x4 slice. The times are simulated.
32 devices in a mesh: rep: 8 (over y, x, core), shard: 4 (over z).
Axes of the slice: x: 2, y: 2, z: 4, core: 2. Of those that a mesh axis runs over, the one named last changes fastest.
Arguments:
- gradients: bfloat16 [8, 96, 2560], P(None, 'shard')
- momentum: float32 [8, 96, 2560], P(None, 'shard'), may hold values from -60 to 60
Outputs:
- updates: bfloat16 [8, 96, 2560], P(None, 'shard', 'rep')
- new_momentum: float32 [8, 96, 2560], P(None, 'shard')
All inputs are finite; a program needn't handle non-finite values.
Results may differ from a plain program's by a relative error of at most 0.0014.
Values may be sent and summed in bfloat16 or wider, within the bound.
A program may use at most 64 MiB of HBM per device.

v0:
```python
import math
import jax
import jax.numpy as jnp
from jax import lax
from jax.sharding import PartitionSpec as P

E = 96
D = 2560
ITERS = 5
momentum_decay = 0.95
norm_floor = 1e-07
quintic_terms = (3.4445, -4.775, 2.0315)


def broadcast(x, axis, root):
    mine = lax.axis_index(axis) == root
    return lax.psum(jnp.where(mine, x, jnp.zeros_like(x)), axis)


def batched_schulz(effective):
    totals = jnp.sqrt(jnp.sum(effective * effective, axis=(1, 2), keepdims=True))
    iterate = effective / (totals + norm_floor)
    for turn in range(ITERS):
        gram_mat = jnp.einsum("kij,klj->kil", iterate, iterate, precision=lax.Precision.HIGHEST)
        square_mat = jnp.einsum("kij,kjl->kil", gram_mat, gram_mat, precision=lax.Precision.HIGHEST)
        poly_mat = quintic_terms[1] * gram_mat + quintic_terms[2] * square_mat
        iterate = quintic_terms[0] * iterate + jnp.einsum(
            "kij,kjl->kil", poly_mat, iterate, precision=lax.Precision.HIGHEST
        )
    return iterate


def per_device(gradients, momentum):
    update_scale = 0.2 * math.sqrt(max(E, D))
    gradient_values = gradients.astype(jnp.float32)
    new_momentum = momentum_decay * momentum + gradient_values
    effective_rows = gradient_values + momentum_decay * new_momentum
    effective = lax.all_to_all(effective_rows, "shard", split_axis=0, concat_axis=1, tiled=True)
    slot_count = effective.shape[0]
    replicas = lax.axis_size("rep")
    column = lax.axis_index("shard")
    replica = lax.axis_index("rep")
    slot_owners = (column * slot_count + jnp.arange(slot_count, dtype=jnp.int32)) % replicas
    owned = slot_owners == replica

    def compute_update(operand):
        return (update_scale * batched_schulz(operand)).astype(jnp.bfloat16)

    def skip_update(operand):
        return jnp.zeros(operand.shape, jnp.bfloat16)

    local_updates = lax.cond(jnp.any(owned), compute_update, skip_update, effective)
    copies = []
    for slot_index in range(slot_count):
        copies.append(broadcast(local_updates[slot_index], "rep", slot_owners[slot_index]))
    stacked = jnp.stack(copies)
    result_rows = lax.all_to_all(stacked, "shard", split_axis=1, concat_axis=0, tiled=True)
    col_width = result_rows.shape[2] // replicas
    kept_cols = lax.dynamic_slice_in_dim(result_rows, replica * col_width, col_width, 2)
    return (kept_cols, new_momentum)


def solution(mesh):
    in_specs = (P(None, "shard", None), P(None, "shard", None))
    out_specs = (P(None, "shard", "rep"), P(None, "shard", None))
    return jax.shard_map(
        per_device, mesh=mesh, in_specs=in_specs, out_specs=out_specs, check_vma=False
    )
```

profile of v0, /device:TPU:0, one launch (start us, length us, event | category | flops | bytes accessed | tf_op | source)
XLA Modules:
  0.0 180.7 jit_solution(16023603056860702382)
XLA Ops:
  7.2 4.4 %convert_add_fusion = (f32[8,24,2560]{2,1,0:T(8,128)}, f32[8,24,2560]{2,1,0:T(8,128)}) fusion(bf16[8,24,2560]{2,1,0:T(8,128)(2,1)} %param.4, f32[8,24,2560]{2,1,0:T(8,128)} %param.5), kind=kLoop, calls=%fused_computation.22 | loop fusion | flops 2457600 | bytes 6881280 | tf_op jit(solution)/shard_map/add | solution.py:37
  11.5 6.3 %all-to-all-start = ((f32[8,24,2560]{2,1,0:T(8,128)}), f32[8,24,2560]{2,1,0:T(8,128)S(1)}, u32[]{:S(2)}, u32[]{:S(2)}) async-start(f32[8,24,2560]{2,1,0:T(8,128)} %get-tuple-element.20), calls=%async_computation | async-start | bytes 3932160 | tf_op jit(solution)/shard_map/all_to_all | solution.py:38
  17.8 0.0 all-reduce.3.cloned.1.call-start
  17.8 0.6 compare_reduce_fusion
  19.2 0.6 fusion.8
  20.9 42.3 %all-to-all-done = f32[8,24,2560]{2,1,0:T(8,128)S(1)} async-done(((f32[8,24,2560]{2,1,0:T(8,128)}), f32[8,24,2560]{2,1,0:T(8,128)S(1)}, u32[]{:S(2)}, u32[]{:S(2)}) %all-to-all-start) | async-done | bytes 1966112 | tf_op jit(solution)/shard_map/all_to_all | solution.py:38
  63.2 0.1 copy.13
  63.4 21.7 %conditional.1 = (bf16[96,2560]{1,0:T(8,128)(2,1)S(1)}, bf16[96,2560]{1,0:T(8,128)(2,1)S(1)}) conditional(s32[]{:T(128)} %convert_element_type.10, () %tuple.22, f32[2,4,24,2560]{3,2,1,0:T(8,128)S(1)} %bitcast.50), branch_computations={%region_1.2_spmd, %region_2.4_spmd} | conditional | flops 5776128000 | bytes 37847088 | solution.py:52
  63.4 0.4 multiply_reduce_fusion
  63.8 0.3 bitcast_divide_fusion
  64.1 1.9 %fusion.9 = f32[2,96,96]{2,1,0:T(8,128)S(1)} fusion(f32[2,96,2560]{2,1,0:T(8,128)S(1)} %bitcast_divide_fusion), kind=kOutput, calls=%fused_computation.35 | convolution fusion | flops 566231040 | bytes 2039808 | tf_op jit(solution)/shard_map/cond/branch_1_fun/kij,klj->kil/dot_general | solution.py:24
  66.0 0.2 fusion.2
  66.2 1.9 %convolution_add_fusion.4 = f32[2,96,2560]{2,1,0:T(8,128)S(1)} fusion(f32[2,96,96]{2,1,0:T(8,128)S(1)} %fusion.2, f32[2,96,2560]{2,1,0:T(8,128)S(1)} %bitcast_divide_fusion), kind=kOutput, calls=%fused_computation.5 | convolution fusion | flops 567214080 | bytes 4005888 | tf_op jit(solution)/shard_map/cond/branch_1_fun/kij,kjl->kil/dot_general | solution.py:27
  68.2 1.9 %fusion.10 = f32[2,96,96]{2,1,0:T(8,128)S(1)} fusion(f32[2,96,2560]{2,1,0:T(8,128)S(1)} %convolution_add_fusion.4), kind=kOutput, calls=%fused_computation.36 | convolution fusion | flops 566231040 | bytes 2039808 | tf_op jit(solution)/shard_map/cond/branch_1_fun/kij,klj->kil/dot_general | solution.py:24
  70.1 0.2 fusion.3
  70.3 1.9 %convolution_add_fusion.3 = f32[2,96,2560]{2,1,0:T(8,128)S(1)} fusion(f32[2,96,96]{2,1,0:T(8,128)S(1)} %fusion.3, f32[2,96,2560]{2,1,0:T(8,128)S(1)} %convolution_add_fusion.4), kind=kOutput, calls=%fused_computation.4 | convolution fusion | flops 567214080 | bytes 4005888 | tf_op jit(solution)/shard_map/cond/branch_1_fun/kij,kjl->kil/dot_general | solution.py:27
  72.3 1.9 %fusion.11 = f32[2,96,96]{2,1,0:T(8,128)S(1)} fusion(f32[2,96,2560]{2,1,0:T(8,128)S(1)} %convolution_add_fusion.3), kind=kOutput, calls=%fused_computation.37 | convolution fusion | flops 566231040 | bytes 2039808 | tf_op jit(solution)/shard_map/cond/branch_1_fun/kij,klj->kil/dot_general | solution.py:24
  74.2 0.2 fusion.4
  74.4 1.9 %convolution_add_fusion.2 = f32[2,96,2560]{2,1,0:T(8,128)S(1)} fusion(f32[2,96,96]{2,1,0:T(8,128)S(1)} %fusion.4, f32[2,96,2560]{2,1,0:T(8,128)S(1)} %convolution_add_fusion.3), kind=kOutput, calls=%fused_computation.3 | convolution fusion | flops 567214080 | bytes 4005888 | tf_op jit(solution)/shard_map/cond/branch_1_fun/kij,kjl->kil/dot_general | solution.py:27
  76.4 2.1 %fusion.12 = f32[2,96,96]{2,1,0:T(8,128)S(1)} fusion(f32[2,96,2560]{2,1,0:T(8,128)S(1)} %convolution_add_fusion.2), kind=kOutput, calls=%fused_computation.38 | convolution fusion | flops 566231040 | bytes 2039808 | tf_op jit(solution)/shard_map/cond/branch_1_fun/kij,klj->kil/dot_general | solution.py:24
  78.4 0.2 fusion.5
  78.7 1.9 %convolution_add_fusion.1 = f32[2,96,2560]{2,1,0:T(8,128)S(1)} fusion(f32[2,96,96]{2,1,0:T(8,128)S(1)} %fusion.5, f32[2,96,2560]{2,1,0:T(8,128)S(1)} %convolution_add_fusion.2), kind=kOutput, calls=%fused_computation.2 | convolution fusion | flops 567214080 | bytes 4005888 | tf_op jit(solution)/shard_map/cond/branch_1_fun/kij,kjl->kil/dot_general | solution.py:27
  80.6 1.9 %fusion.13 = f32[2,96,96]{2,1,0:T(8,128)S(1)} fusion(f32[2,96,2560]{2,1,0:T(8,128)S(1)} %convolution_add_fusion.1), kind=kOutput, calls=%fused_computation.39 | convolution fusion | flops 566231040 | bytes 2039808 | tf_op jit(solution)/shard_map/cond/branch_1_fun/kij,klj->kil/dot_general | solution.py:24
  82.5 0.2 fusion.6
  82.8 2.0 %fusion.1 = bf16[2,96,2560]{2,1,0:T(8,128)(2,1)S(1)} fusion(f32[2,96,96]{2,1,0:T(8,128)S(1)} %fusion.6, f32[2,96,2560]{2,1,0:T(8,128)S(1)} %convolution_add_fusion.1), kind=kOutput, calls=%fused_computation.6 | convolution fusion | flops 568197120 | bytes 3022848 | tf_op jit(solution)/shard_map/cond/branch_1_fun/kij,kjl->kil/dot_general | solution.py:27
  84.8 0.1 slice_bitcast_fusion
  85.1 1.1 select_bitcast_fusion
  86.2 0.0 all-reduce.3.cloned.1.call-update
  86.2 55.7 %all-reduce.3.cloned.1.call-done = (bf16[1,96,2560]{2,1,0:T(8,128)(2,1)}, bf16[1,96,2560]{2,1,0:T(8,128)(2,1)}) async-done(((bf16[1,96,2560]{2,1,0:T(8,128)(2,1)}, bf16[1,96,2560]{2,1,0:T(8,128)(2,1)}), (bf16[1,96,2560]{2,1,0:T(8,128)(2,1)}, bf16[1,96,2560]{2,1,0:T(8,128)(2,1)})) %all-reduce.3.cloned.1.call-update) | async-done | bytes 983056 | tf_op jit(solution)/shard_map/psum | solution.py:17
  141.8 1.3 pad_maximum_fusion
  143.1 2.0 %copy.10 = bf16[2,96,2560]{2,0,1:T(2,128)(2,1)} copy(bf16[2,96,2560]{2,1,0:T(8,128)(2,1)S(1)} %pad_maximum_fusion) | data formatting | bytes 1966080 | tf_op jit(solution)/shard_map/stack | solution.py:56
  145.1 4.4 %all-to-all-start.1 = ((bf16[2,96,2560]{2,0,1:T(2,128)(2,1)}), bf16[2,96,2560]{2,0,1:T(2,128)(2,1)S(1)}, u32[]{:S(2)}, u32[]{:S(2)}) async-start(bf16[2,96,2560]{2,0,1:T(2,128)(2,1)} %copy.10), calls=%async_computation.1 | async-start | bytes 1966080 | tf_op jit(solution)/shard_map/all_to_all | solution.py:57
  149.5 23.4 %all-to-all-done.1 = bf16[2,96,2560]{2,0,1:T(2,128)(2,1)S(1)} async-done(((bf16[2,96,2560]{2,0,1:T(2,128)(2,1)}), bf16[2,96,2560]{2,0,1:T(2,128)(2,1)S(1)}, u32[]{:S(2)}, u32[]{:S(2)}) %all-to-all-start.1) | async-done | bytes 983072 | tf_op jit(solution)/shard_map/all_to_all | solution.py:57
  173.0 0.1 copy.11
  173.1 0.8 constant_dynamic-slice_fusion
  (2 shorter events, 0.0 us)
Async XLA Ops:
  11.5 51.7 %all-to-all-start = ((f32[8,24,2560]{2,1,0:T(8,128)}), f32[8,24,2560]{2,1,0:T(8,128)S(1)}, u32[]{:S(2)}, u32[]{:S(2)}) async-start(f32[8,24,2560]{2,1,0:T(8,128)} %get-tuple-element.20), calls=%async_computation | async-start | bytes 3932160 | tf_op jit(solution)/shard_map/all_to_all | solution.py:38
  17.8 124.0 %all-reduce.3.cloned.1.call-start = ((), (), s32[]{:S(2)}) async-start(), calls=%async_computation.2 | async-start | bytes 1966080 | tf_op jit(solution)/shard_map/psum | solution.py:17
  145.1 27.9 %all-to-all-start.1 = ((bf16[2,96,2560]{2,0,1:T(2,128)(2,1)}), bf16[2,96,2560]{2,0,1:T(2,128)(2,1)S(1)}, u32[]{:S(2)}, u32[]{:S(2)}) async-start(bf16[2,96,2560]{2,0,1:T(2,128)(2,1)} %copy.10), calls=%async_computation.1 | async-start | bytes 1966080 | tf_op jit(solution)/shard_map/all_to_all | solution.py:57
Sparse Core Ops, SparseCore 0:
  86.3 55.4 all-reduce.2
where the time goes:
time: 181 us
  waiting for transfers between devices  121 us (67%)
  matrix products  20.6 us (11%)
  between operations  15.9 us (9%)
  starting transfers between devices  10.8 us (6%)
  other arithmetic  8.01 us (4%)
  local copies, waits for them, and re-layouts  3.64 us (2%)
    psum x1, waiting for transfers between devices, broadcast(): return lax.psum(jnp.where(mine, x, jnp.zeros_like(x)), axis)  55.7 us
    all_to_all x1, waiting for transfers between devices, per_device(): lax.all_to_all(effective_rows, 'shard', split_axis=0, concat_axis=1, tile...  42.3 us
    all_to_all x1, waiting for transfers between devices, per_device(): lax.all_to_all(stacked, 'shard', split_axis=1, concat_axis=0, tiled=True)  23.4 us
    dot_general x5, matrix products, batched_schulz(): jnp.einsum('kij,kjl->kil', poly_mat, iterate, precision=lax.Precision.HIG...  9.76 us
    dot_general x5, matrix products, batched_schulz(): jnp.einsum('kij,klj->kil', iterate, iterate, precision=lax.Precision.HIGH...  9.67 us
    all_to_all x1, starting transfers between devices, per_device(): lax.all_to_all(effective_rows, 'shard', split_axis=0, concat_axis=1, tile...  6.32 us
    all_to_all x1, starting transfers between devices, per_device(): lax.all_to_all(stacked, 'shard', split_axis=1, concat_axis=0, tiled=True)  4.45 us
    add x1, other arithmetic, per_device(): effective_rows = gradient_values + momentum_decay * new_momentum  4.36 us
  transfers between devices with their start and end apart: 3, of which 3 were waited for; matrix products, arithmetic and copies ran while one was open for 1% of the time, Pallas kernels for 0%

commit v1 on v0

--- a/solution.py
+++ b/solution.py
@@ -10,6 +10,18 @@
 momentum_decay = 0.95
 norm_floor = 1e-07
 quintic_terms = (3.4445, -4.775, 2.0315)
+
+
+def exchange_directly(array, axis, split, join):
+    ways, here = (lax.axis_size(axis), lax.axis_index(axis))
+    width = array.shape[split] // ways
+    turned = jnp.roll(array, -here * width, axis=split)
+    got = [lax.slice_in_dim(turned, 0, width, axis=split)]
+    for far in range(1, ways):
+        sent = lax.slice_in_dim(turned, far * width, (far + 1) * width, axis=split)
+        got.append(lax.ppermute(sent, axis, [(d, (d + far) % ways) for d in range(ways)]))
+    line = jnp.concatenate(got[::-1], axis=join)
+    return jnp.roll(line, (here + 1) * got[0].shape[join], axis=join)
 
 
 def broadcast(x, axis, root):
@@ -54,7 +66,7 @@
     for slot_index in range(slot_count):
         copies.append(broadcast(local_updates[slot_index], "rep", slot_owners[slot_index]))
     stacked = jnp.stack(copies)
-    result_rows = lax.all_to_all(stacked, "shard", split_axis=1, concat_axis=0, tiled=True)
+    result_rows = exchange_directly(stacked, "shard", 1, 0)
     col_width = result_rows.shape[2] // replicas
     kept_cols = lax.dynamic_slice_in_dim(result_rows, replica * col_width, col_width, 2)
     return (kept_cols, new_momentum)

time: 181 us -> 175 us (0.967)
  waiting for transfers between devices: 121 us -> 117 us
  local copies, waits for them, and re-layouts: 3.64 us -> 1.76 us
    all_to_all x1 -> x0, waiting for transfers between devices: 23.4 us -> none  [per_device(): lax.all_to_all(stacked, 'shard', split_axis=1, concat_axis=0, tiled=True)]
    ppermute x0 -> x3, waiting for transfers between devices: none -> 19 us  [exchange_directly(): lax.ppermute(sent, axis, [(d, (d + far) % ways) for d in range(ways)])]
    all_to_all x1 -> x0, starting transfers between devices: 4.45 us -> none  [per_device(): lax.all_to_all(stacked, 'shard', split_axis=1, concat_axis=0, tiled=True)]
    ppermute x0 -> x3, starting transfers between devices: none -> 4.4 us  [exchange_directly(): lax.ppermute(sent, axis, [(d, (d + far) % ways) for d in range(ways)])]
    another operation x1 -> x0, local copies, waits for them, and re-layouts: 1.97 us -> none  [per_device(): stacked = jnp.stack(copies)]
    concatenate x0 -> x1, other arithmetic: none -> 1.83 us  [exchange_directly(): turned = jnp.roll(array, -here * width, axis=split)]
  transfers between devices with their start and end apart: 3 -> 5, of which waited for: 3 -> 4; matrix products, arithmetic and copies ran while one was open for 1% -> 1% of each run, Pallas kernels for 0% -> 0%
where the time goes in v1:
time: 175 us
  waiting for transfers between devices  117 us (67%)
  matrix products  20.6 us (12%)
  between operations  16.1 us (9%)
  starting transfers between devices  10.7 us (6%)
  other arithmetic  8.59 us (5%)
  local copies, waits for them, and re-layouts  1.76 us (1%)
    psum x1, waiting for transfers between devices, broadcast(): return lax.psum(jnp.where(mine, x, jnp.zeros_like(x)), axis)  55.6 us
    all_to_all x1, waiting for transfers between devices, per_device(): lax.all_to_all(effective_rows, 'shard', split_axis=0, concat_axis=1, tile...  42.2 us
    ppermute x3, waiting for transfers between devices, exchange_directly(): lax.ppermute(sent, axis, [(d, (d + far) % ways) for d in range(ways)])  19 us
    dot_general x5, matrix products, batched_schulz(): jnp.einsum('kij,kjl->kil', poly_mat, iterate, precision=lax.Precision.HIG...  9.76 us
    dot_general x5, matrix products, batched_schulz(): jnp.einsum('kij,klj->kil', iterate, iterate, precision=lax.Precision.HIGH...  9.67 us
    all_to_all x1, starting transfers between devices, per_device(): lax.all_to_all(effective_rows, 'shard', split_axis=0, concat_axis=1, tile...  6.32 us
    ppermute x3, starting transfers between devices, exchange_directly(): lax.ppermute(sent, axis, [(d, (d + far) % ways) for d in range(ways)])  4.4 us
    add x1, other arithmetic, per_device(): effective_rows = gradient_values + momentum_decay * new_momentum  4.37 us
  transfers between devices with their start and end apart: 5, of which 4 were waited for; matrix products, arithmetic and copies ran while one was open for 1% of the time, Pallas kernels for 0%

profile of v1, /device:TPU:0, one launch (start us, length us, event | category | flops | bytes accessed | tf_op | source)
XLA Modules:
  0.0 175.0 jit_solution(11043039784954570169)
XLA Ops:
  7.2 4.4 %convert_add_fusion = (f32[8,24,2560]{2,1,0:T(8,128)}, f32[8,24,2560]{2,1,0:T(8,128)}) fusion(bf16[8,24,2560]{2,1,0:T(8,128)(2,1)} %param.4, f32[8,24,2560]{2,1,0:T(8,128)} %param.5), kind=kLoop, calls=%fused_computation.22 | loop fusion | flops 2457600 | bytes 6881280 | tf_op jit(solution)/shard_map/add | solution.py:49
  11.5 6.3 %all-to-all-start = ((f32[8,24,2560]{2,1,0:T(8,128)}), f32[8,24,2560]{2,1,0:T(8,128)S(1)}, u32[]{:S(2)}, u32[]{:S(2)}) async-start(f32[8,24,2560]{2,1,0:T(8,128)} %get-tuple-element.20), calls=%async_computation | async-start | bytes 3932160 | tf_op jit(solution)/shard_map/all_to_all | solution.py:50
  17.9 0.0 all-reduce.3.cloned.1.call-start
  17.9 0.6 compare_reduce_fusion
  19.2 0.6 fusion.12
  21.0 42.2 %all-to-all-done = f32[8,24,2560]{2,1,0:T(8,128)S(1)} async-done(((f32[8,24,2560]{2,1,0:T(8,128)}), f32[8,24,2560]{2,1,0:T(8,128)S(1)}, u32[]{:S(2)}, u32[]{:S(2)}) %all-to-all-start) | async-done | bytes 1966112 | tf_op jit(solution)/shard_map/all_to_all | solution.py:50
  63.2 0.1 copy.6
  63.4 21.7 %conditional.1 = (bf16[96,2560]{1,0:T(8,128)(2,1)S(1)}, bf16[96,2560]{1,0:T(8,128)(2,1)S(1)}) conditional(s32[]{:T(128)} %convert_element_type.10, () %tuple.22, f32[2,4,24,2560]{3,2,1,0:T(8,128)S(1)} %bitcast.46), branch_computations={%region_1.2_spmd, %region_2.4_spmd} | conditional | flops 5776128000 | bytes 37847088 | solution.py:64
  63.4 0.4 multiply_reduce_fusion
  63.8 0.3 bitcast_divide_fusion
  64.1 1.9 %fusion.13 = f32[2,96,96]{2,1,0:T(8,128)S(1)} fusion(f32[2,96,2560]{2,1,0:T(8,128)S(1)} %bitcast_divide_fusion), kind=kOutput, calls=%fused_computation.50 | convolution fusion | flops 566231040 | bytes 2039808 | tf_op jit(solution)/shard_map/cond/branch_1_fun/kij,klj->kil/dot_general | solution.py:36
  66.0 0.2 fusion.2
  66.2 1.9 %convolution_add_fusion.4 = f32[2,96,2560]{2,1,0:T(8,128)S(1)} fusion(f32[2,96,96]{2,1,0:T(8,128)S(1)} %fusion.2, f32[2,96,2560]{2,1,0:T(8,128)S(1)} %bitcast_divide_fusion), kind=kOutput, calls=%fused_computation.5 | convolution fusion | flops 567214080 | bytes 4005888 | tf_op jit(solution)/shard_map/cond/branch_1_fun/kij,kjl->kil/dot_general | solution.py:39
  68.2 1.9 %fusion.14 = f32[2,96,96]{2,1,0:T(8,128)S(1)} fusion(f32[2,96,2560]{2,1,0:T(8,128)S(1)} %convolution_add_fusion.4), kind=kOutput, calls=%fused_computation.51 | convolution fusion | flops 566231040 | bytes 2039808 | tf_op jit(solution)/shard_map/cond/branch_1_fun/kij,klj->kil/dot_general | solution.py:36
  70.1 0.2 fusion.3
  70.3 1.9 %convolution_add_fusion.3 = f32[2,96,2560]{2,1,0:T(8,128)S(1)} fusion(f32[2,96,96]{2,1,0:T(8,128)S(1)} %fusion.3, f32[2,96,2560]{2,1,0:T(8,128)S(1)} %convolution_add_fusion.4), kind=kOutput, calls=%fused_computation.4 | convolution fusion | flops 567214080 | bytes 4005888 | tf_op jit(solution)/shard_map/cond/branch_1_fun/kij,kjl->kil/dot_general | solution.py:39
  72.3 1.9 %fusion.15 = f32[2,96,96]{2,1,0:T(8,128)S(1)} fusion(f32[2,96,2560]{2,1,0:T(8,128)S(1)} %convolution_add_fusion.3), kind=kOutput, calls=%fused_computation.52 | convolution fusion | flops 566231040 | bytes 2039808 | tf_op jit(solution)/shard_map/cond/branch_1_fun/kij,klj->kil/dot_general | solution.py:36
  74.2 0.2 fusion.4
  74.4 1.9 %convolution_add_fusion.2 = f32[2,96,2560]{2,1,0:T(8,128)S(1)} fusion(f32[2,96,96]{2,1,0:T(8,128)S(1)} %fusion.4, f32[2,96,2560]{2,1,0:T(8,128)S(1)} %convolution_add_fusion.3), kind=kOutput, calls=%fused_computation.3 | convolution fusion | flops 567214080 | bytes 4005888 | tf_op jit(solution)/shard_map/cond/branch_1_fun/kij,kjl->kil/dot_general | solution.py:39
  76.4 2.1 %fusion.16 = f32[2,96,96]{2,1,0:T(8,128)S(1)} fusion(f32[2,96,2560]{2,1,0:T(8,128)S(1)} %convolution_add_fusion.2), kind=kOutput, calls=%fused_computation.53 | convolution fusion | flops 566231040 | bytes 2039808 | tf_op jit(solution)/shard_map/cond/branch_1_fun/kij,klj->kil/dot_general | solution.py:36
  78.5 0.2 fusion.5
  78.7 1.9 %convolution_add_fusion.1 = f32[2,96,2560]{2,1,0:T(8,128)S(1)} fusion(f32[2,96,96]{2,1,0:T(8,128)S(1)} %fusion.5, f32[2,96,2560]{2,1,0:T(8,128)S(1)} %convolution_add_fusion.2), kind=kOutput, calls=%fused_computation.2 | convolution fusion | flops 567214080 | bytes 4005888 | tf_op jit(solution)/shard_map/cond/branch_1_fun/kij,kjl->kil/dot_general | solution.py:39
  80.7 1.9 %fusion.17 = f32[2,96,96]{2,1,0:T(8,128)S(1)} fusion(f32[2,96,2560]{2,1,0:T(8,128)S(1)} %convolution_add_fusion.1), kind=kOutput, calls=%fused_computation.54 | convolution fusion | flops 566231040 | bytes 2039808 | tf_op jit(solution)/shard_map/cond/branch_1_fun/kij,klj->kil/dot_general | solution.py:36
  82.6 0.2 fusion.6
  82.8 2.0 %fusion.1 = bf16[2,96,2560]{2,1,0:T(8,128)(2,1)S(1)} fusion(f32[2,96,96]{2,1,0:T(8,128)S(1)} %fusion.6, f32[2,96,2560]{2,1,0:T(8,128)S(1)} %convolution_add_fusion.1), kind=kOutput, calls=%fused_computation.6 | convolution fusion | flops 568197120 | bytes 3022848 | tf_op jit(solution)/shard_map/cond/branch_1_fun/kij,kjl->kil/dot_general | solution.py:39
  84.8 0.1 slice_bitcast_fusion
  85.1 1.1 select_bitcast_fusion
  86.2 0.0 all-reduce.3.cloned.1.call-update
  86.2 55.6 %all-reduce.3.cloned.1.call-done = (bf16[1,96,2560]{2,1,0:T(8,128)(2,1)}, bf16[1,96,2560]{2,1,0:T(8,128)(2,1)}) async-done(((bf16[1,96,2560]{2,1,0:T(8,128)(2,1)}, bf16[1,96,2560]{2,1,0:T(8,128)(2,1)}), (bf16[1,96,2560]{2,1,0:T(8,128)(2,1)}, bf16[1,96,2560]{2,1,0:T(8,128)(2,1)})) %all-reduce.3.cloned.1.call-update) | async-done | bytes 983056 | tf_op jit(solution)/shard_map/psum | solution.py:29
  141.9 1.8 %fusion.8 = bf16[2,96,2560]{2,1,0:T(8,128)(2,1)S(1)} fusion(s32[]{:T(128)S(6)} %select_n.56, bf16[1,96,2560]{2,1,0:T(8,128)(2,1)} %get-tuple-element.18, bf16[1,96,2560]{2,1,0:T(8,128)(2,1)} %get-tuple-element.19), kind=kLoop, calls=%fused_computation.30 | loop fusion | flops 3932160 | bytes 1966084 | tf_op jit(solution)/shard_map/jit(_roll_dynamic)/concatenate | solution.py:18
  143.7 0.1 fusion.11
  143.7 3.3 %collective-permute-start = (bf16[2,24,2560]{2,1,0:T(8,128)(2,1)S(1)}, bf16[2,24,2560]{2,1,0:T(8,128)(2,1)S(1)}, u32[]{:S(2)}, u32[]{:S(2)}) collective-permute-start(bf16[2,24,2560]{2,1,0:T(8,128)(2,1)S(1)} %get-tuple-element.26), channel_id=1, source_target_pairs={{0,3},{1,0},{2,1},{3,2},{4,7},{5,4},{6,5},{7,6},{8,11},{9,8},{10,9... | collective-permute-start | bytes 737288 | tf_op jit(solution)/shard_map/ppermute | solution.py:22
  147.0 0.0 collective-permute-start.1
  147.0 1.1 collective-permute-start.2
  148.1 5.3 %collective-permute-done = bf16[2,24,2560]{2,1,0:T(8,128)(2,1)S(1)} collective-permute-done((bf16[2,24,2560]{2,1,0:T(8,128)(2,1)S(1)}, bf16[2,24,2560]{2,1,0:T(8,128)(2,1)S(1)}, u32[]{:S(2)}, u32[]{:S(2)}) %collective-permute-start) | collective-permute-done | bytes 245792 | tf_op jit(solution)/shard_map/ppermute | solution.py:22
  153.5 13.7 %collective-permute-done.1 = bf16[2,24,2560]{2,1,0:T(8,128)(2,1)S(1)} collective-permute-done((bf16[2,24,2560]{2,1,0:T(8,128)(2,1)S(1)}, bf16[2,24,2560]{2,1,0:T(8,128)(2,1)S(1)}, u32[]{:S(2)}, u32[]{:S(2)}) %collective-permute-start.1) | collective-permute-done | bytes 245792 | tf_op jit(solution)/shard_map/ppermute | solution.py:22
  167.2 0.0 collective-permute-done.2
  167.4 0.8 constant_dynamic-slice_fusion
  (10 shorter events, 0.2 us)
Async XLA Ops:
  11.5 51.7 %all-to-all-start = ((f32[8,24,2560]{2,1,0:T(8,128)}), f32[8,24,2560]{2,1,0:T(8,128)S(1)}, u32[]{:S(2)}, u32[]{:S(2)}) async-start(f32[8,24,2560]{2,1,0:T(8,128)} %get-tuple-element.20), calls=%async_computation | async-start | bytes 3932160 | tf_op jit(solution)/shard_map/all_to_all | solution.py:50
  17.9 124.0 %all-reduce.3.cloned.1.call-start = ((), (), s32[]{:S(2)}) async-start(), calls=%async_computation.1 | async-start | bytes 1966080 | tf_op jit(solution)/shard_map/psum | solution.py:29
  143.7 9.7 %collective-permute-start = (bf16[2,24,2560]{2,1,0:T(8,128)(2,1)S(1)}, bf16[2,24,2560]{2,1,0:T(8,128)(2,1)S(1)}, u32[]{:S(2)}, u32[]{:S(2)}) collective-permute-start(bf16[2,24,2560]{2,1,0:T(8,128)(2,1)S(1)} %get-tuple-element.26), channel_id=1, source_target_pairs={{0,3},{1,0},{2,1},{3,2},{4,7},{5,4},{6,5},{7,6},{8,11},{9,8},{10,9... | collective-permute-start | bytes 737288 | tf_op jit(solution)/shard_map/ppermute | solution.py:22
  147.0 20.2 %collective-permute-start.1 = (bf16[2,24,2560]{2,1,0:T(8,128)(2,1)S(1)}, bf16[2,24,2560]{2,1,0:T(8,128)(2,1)S(1)}, u32[]{:S(2)}, u32[]{:S(2)}) collective-permute-start(bf16[2,24,2560]{2,1,0:T(8,128)(2,1)S(1)} %get-tuple-element.25), channel_id=1, source_target_pairs={{0,2},{1,3},{2,0},{3,1},{4,6},{5,7},{6,4},{7,5},{8,10},{9,11},{10,... | collective-permute-start | bytes 737288 | tf_op jit(solution)/shard_map/ppermute | solution.py:22
  147.0 20.2 %collective-permute-start.2 = (bf16[2,24,2560]{2,1,0:T(8,128)(2,1)S(1)}, bf16[2,24,2560]{2,1,0:T(8,128)(2,1)S(1)}, u32[]{:S(2)}, u32[]{:S(2)}) collective-permute-start(bf16[2,24,2560]{2,1,0:T(8,128)(2,1)S(1)} %get-tuple-element.24), channel_id=1, source_target_pairs={{0,1},{1,2},{2,3},{3,0},{4,5},{5,6},{6,7},{7,4},{8,9},{9,10},{10,1... | collective-permute-start | bytes 737288 | tf_op jit(solution)/shard_map/ppermute | solution.py:22
Sparse Core Ops, SparseCore 0:
  86.3 55.4 all-reduce.2
